TPU v7x, 32 devices: a whole 2x2x4 slice. The times are simulated.
32 devices in a mesh: modes: 4 (over y, x), atoms: 8 (over z, core).
Axes of the slice: x: 2, y: 2, z: 4, core: 2. Of those that a mesh axis runs over, the one named last changes fastest.
Arguments:
- left_modes: bfloat16 [3, 8192, 3072], P(None, 'atoms', 'modes'), may hold values from -6 to 6
- right_panel: bfloat16 [3, 8192, 256], P(None, 'atoms', 'modes'), may hold values from -6 to 6
- force_blocks: float32 [3, 3, 16, 8192], P(None, None, None, 'atoms'), may hold values from -0.875 to 0.875
- bond_vectors: float32 [3, 16, 8192], P(None, None, 'atoms'), may hold values from -1 to 1
- neighbours: int32 [16, 8192], P(None, 'atoms'), may hold values from 0 to 8191, as said below
- counts: int32 [8192], P('atoms'), may hold values from 1 to 16
- left_bins: int32 [3072], P(('modes', 'atoms')), may hold values from 1 to 32
- right_bins: int32 [256], replicated, may hold values from 1 to 32
Outputs:
- diffusivity: float32 [3072], P(('modes', 'atoms'))
Inputs may be any that keep to these rules, and one draw needn't show every extreme that they name: neighbours[k, a] = (a + s) modulo 8192 with 1 <= |s| <= 256; some entry has |s| = 256.
All inputs are finite; a program needn't handle non-finite values.
Results may differ from a plain program's by a relative error of at most 0.00058.
Values may be sent and summed in bfloat16 or wider, within the bound.
A program may use at most 128 MiB of HBM per device.

v0:
```python
import math

import jax
import jax.numpy as jnp
from jax import lax
from jax.sharding import PartitionSpec as P

omega_step = 0.05
gamma = 0.1


def with_halo(block, sides, width):
    for axis, dim in sides:
        count = lax.axis_size(axis)
        forward = [(i, i + 1) for i in range(count - 1)]
        forward.append((count - 1, 0))
        backward = [(target, source) for source, target in forward]
        low = lax.ppermute(
            lax.slice_in_dim(block, block.shape[dim] - width, None, axis=dim), axis, forward
        )
        high = lax.ppermute(lax.slice_in_dim(block, 0, width, axis=dim), axis, backward)
        block = jnp.concatenate([low, block, high], axis=dim)
    return block


def operator_blocks(force_blocks, bond_vectors, counts):
    slot_ids = lax.broadcasted_iota(jnp.int32, bond_vectors.shape[1:], 0)
    live_slot = (slot_ids < counts[None, :]).astype(jnp.float32)
    scaled = bond_vectors * live_slot[None]
    return (scaled[:, None, None, :, :] * force_blocks[None]).astype(jnp.bfloat16)


def apply_flux(extended, blocks, local_index):
    atoms_dev = local_index.shape[1]
    block_width = math.gcd(atoms_dev, 256)
    columns = extended.shape[2]
    zero_flux = jnp.zeros((3, 3, atoms_dev, columns), jnp.bfloat16)

    def one_block(block_step, flux_all):
        start_row = block_step * block_width
        near_index = lax.dynamic_slice_in_dim(local_index, start_row, block_width, 1)
        nearby = extended[:, near_index, :]
        coefficient = lax.dynamic_slice_in_dim(blocks, start_row, block_width, 4)
        block_flux = jnp.einsum(
            "xcdkb,dkbj->xcbj", coefficient, nearby, preferred_element_type=jnp.float32
        )
        return lax.dynamic_update_slice_in_dim(
            flux_all, block_flux.astype(jnp.bfloat16), start_row, 2
        )

    return lax.fori_loop(0, atoms_dev // block_width, one_block, zero_flux)


def per_device(
    left_modes, right_panel, force_blocks, bond_vectors, neighbours, counts, left_bins, right_bins
):
    atoms_dev = right_panel.shape[1]
    reach_rows = atoms_dev // 4
    total_atoms = atoms_dev * lax.axis_size("atoms")
    first_atom = lax.axis_index("atoms") * atoms_dev
    local_index = jnp.mod(neighbours - first_atom + reach_rows, total_atoms)
    blocks = operator_blocks(force_blocks, bond_vectors, counts)
    extended = with_halo(right_panel, (("atoms", 1),), reach_rows)
    flux_all = lax.all_gather(
        apply_flux(extended, blocks, local_index), "modes", axis=3, tiled=True
    )
    left_flat = left_modes.reshape(3 * atoms_dev, left_modes.shape[2])
    panel_cols = flux_all.shape[3]
    flux_flat = flux_all.reshape(3, 3 * atoms_dev, panel_cols)
    owned_sums = lax.psum_scatter(
        lax.dot_general(
            left_flat, flux_flat, (((0,), (1,)), ((), ())), preferred_element_type=jnp.float32
        ),
        "atoms",
        scatter_dimension=0,
        tiled=True,
    )
    squares = jnp.sum(owned_sums * owned_sums, axis=1)
    omega_left = omega_step * left_bins.astype(jnp.float32)
    omega_right = omega_step * right_bins.astype(jnp.float32)
    freq_gap = omega_left[:, None] - omega_right[None, :]
    weight = gamma * gamma / (freq_gap * freq_gap + gamma * gamma)
    weight = (
        weight
        * (omega_left[:, None] + omega_right[None, :]) ** 2
        / (4.0 * omega_left[:, None] * omega_right[None, :])
    )
    return 4.0 * jnp.sum(weight * squares, axis=1) / (total_atoms * panel_cols)


def solution(mesh):
    return jax.shard_map(
        per_device,
        mesh=mesh,
        in_specs=(
            P(None, "atoms", "modes"),
            P(None, "atoms", "modes"),
            P(None, None, None, "atoms"),
            P(None, None, "atoms"),
            P(None, "atoms"),
            P("atoms"),
            P(("modes", "atoms")),
            P(),
        ),
        out_specs=P(("modes", "atoms")),
        check_vma=False,
    )
```

profile of v0, /device:TPU:0, one launch (start us, length us, event | category | flops | bytes accessed | tf_op | source)
XLA Modules:
  0.0 289.6 jit_solution(9142103451836289400)
XLA Ops:
  6.5 1.0 fusion.19
  8.0 4.1 %collective-permute-start.1 = (bf16[3,256,64]{1,2,0:T(8,128)(2,1)S(1)}, bf16[3,256,64]{1,2,0:T(8,128)(2,1)S(1)}, u32[]{:S(2)}, u32[]{:S(2)}) collective-permute-start(bf16[3,256,64]{1,2,0:T(8,128)(2,1)S(1)} %get-tuple-element.116), channel_id=1, source_target_pairs={{1,0},{2,1},{3,2},{4,3},{5,4},{6,5},{7,6},{0,7},{9,8},{10,9},{11,1... | collective-permute-start | bytes 294920 | tf_op jit(solution)/shard_map/ppermute | solution.py:21
  12.1 6.2 %copy.25 = f32[3,3,16,1024]{2,0,1,3:T(4,128)} copy(f32[3,3,16,1024]{3,2,1,0:T(8,128)} %param.12) | data formatting | bytes 1179648 | tf_op args[2]
  18.3 0.8 copy.24
  19.2 12.3 %multiply_convert_fusion = bf16[3,3,3,16,1024]{3,1,2,0,4:T(4,128)(2,1)} fusion(f32[3,3,16,1024]{2,0,1,3:T(4,128)} %copy.25, f32[3,16,1024]{1,0,2:T(4,128)S(1)} %copy.24), kind=kLoop, calls=%fused_computation.12 | loop fusion | flops 884736 | bytes 1671168 | tf_op jit(solution)/shard_map/convert_element_type | solution.py:30
  31.6 1.0 copy.26
  32.6 1.2 broadcast_in_dim.9.clone
  33.8 144.4 %while.13 = (s32[]{:T(128)}, bf16[3,3,1024,64]{2,3,1,0:T(8,128)(2,1)}, s32[16,1024]{1,0:T(8,128)S(1)}, bf16[3,1536,64]{2,0,1:T(4,128)(2,1)S(1)}, bf16[3,3,3,16,1...) while((s32[]{:T(128)}, bf16[3,3,1024,64]{2,3,1,0:T(8,128)(2,1)}, ...), condition=%wide.region_1.2_spmd, body=%wide.region_0.1_spmd.sunk | while | flops 14319622 | bytes 11288727 | solution.py:51
  33.8 28.7 %gather_fusion = bf16[4096,3,64]{2,1,0:T(4,128)(2,1)} fusion(bf16[3,1536,64]{2,0,1:T(4,128)(2,1)S(1)} %get-tuple-element.171, s32[4096]{0:T(1024)S(1)} %broadcast_clamp_fusion.2), kind=kCustom, calls=%fused_computation.clone.1 | custom fusion | bytes 3162112 | tf_op jit(solution)/shard_map/while/body/eval_jaxpr/gather | solution.py:42
  62.5 6.1 %fusion.28 = bf16[3,3,256,64]{3,1,0,2:T(4,128)(2,1)S(1)} fusion(bf16[3,3,3,16,1024]{3,1,2,0,4:T(4,128)(2,1)} %get-tuple-element.172, s32[]{:T(128)S(6)} %select_n.31, bf16[16,256,3,64]{3,2,1,0:T(4,128)(2,1)} %bitcast.46), kind=kOutput, calls=%fused_computation.6.clone.1 | convolution fusion | flops 14303232 | bytes 6848516 | tf_op jit(solution)/shard_map/while/body/eval_jaxpr/xcdkb,dkbj->xcbj/dot_general | solution.py:44
  69.1 0.8 constant_dynamic-update-slice_fusion.2
  70.0 28.7 %gather_fusion = bf16[4096,3,64]{2,1,0:T(4,128)(2,1)} fusion(bf16[3,1536,64]{2,0,1:T(4,128)(2,1)S(1)} %get-tuple-element.171, s32[4096]{0:T(1024)S(1)} %broadcast_clamp_fusion.2), kind=kCustom, calls=%fused_computation.clone.1 | custom fusion | bytes 3162112 | tf_op jit(solution)/shard_map/while/body/eval_jaxpr/gather | solution.py:42
  98.6 6.1 %fusion.28 = bf16[3,3,256,64]{3,1,0,2:T(4,128)(2,1)S(1)} fusion(bf16[3,3,3,16,1024]{3,1,2,0,4:T(4,128)(2,1)} %get-tuple-element.172, s32[]{:T(128)S(6)} %select_n.31, bf16[16,256,3,64]{3,2,1,0:T(4,128)(2,1)} %bitcast.46), kind=kOutput, calls=%fused_computation.6.clone.1 | convolution fusion | flops 14303232 | bytes 6848516 | tf_op jit(solution)/shard_map/while/body/eval_jaxpr/xcdkb,dkbj->xcbj/dot_general | solution.py:44
  105.3 0.8 constant_dynamic-update-slice_fusion.2
  106.1 28.7 %gather_fusion = bf16[4096,3,64]{2,1,0:T(4,128)(2,1)} fusion(bf16[3,1536,64]{2,0,1:T(4,128)(2,1)S(1)} %get-tuple-element.171, s32[4096]{0:T(1024)S(1)} %broadcast_clamp_fusion.2), kind=kCustom, calls=%fused_computation.clone.1 | custom fusion | bytes 3162112 | tf_op jit(solution)/shard_map/while/body/eval_jaxpr/gather | solution.py:42
  134.8 6.1 %fusion.28 = bf16[3,3,256,64]{3,1,0,2:T(4,128)(2,1)S(1)} fusion(bf16[3,3,3,16,1024]{3,1,2,0,4:T(4,128)(2,1)} %get-tuple-element.172, s32[]{:T(128)S(6)} %select_n.31, bf16[16,256,3,64]{3,2,1,0:T(4,128)(2,1)} %bitcast.46), kind=kOutput, calls=%fused_computation.6.clone.1 | convolution fusion | flops 14303232 | bytes 6848516 | tf_op jit(solution)/shard_map/while/body/eval_jaxpr/xcdkb,dkbj->xcbj/dot_general | solution.py:44
  142.2 28.7 %gather_fusion = bf16[4096,3,64]{2,1,0:T(4,128)(2,1)} fusion(bf16[3,1536,64]{2,0,1:T(4,128)(2,1)S(1)} %get-tuple-element.171, s32[4096]{0:T(1024)S(1)} %broadcast_clamp_fusion.2), kind=kCustom, calls=%fused_computation.clone.1 | custom fusion | bytes 3162112 | tf_op jit(solution)/shard_map/while/body/eval_jaxpr/gather | solution.py:42
  170.9 6.1 %fusion.28 = bf16[3,3,256,64]{3,1,0,2:T(4,128)(2,1)S(1)} fusion(bf16[3,3,3,16,1024]{3,1,2,0,4:T(4,128)(2,1)} %get-tuple-element.172, s32[]{:T(128)S(6)} %select_n.31, bf16[16,256,3,64]{3,2,1,0:T(4,128)(2,1)} %bitcast.46), kind=kOutput, calls=%fused_computation.6.clone.1 | convolution fusion | flops 14303232 | bytes 6848516 | tf_op jit(solution)/shard_map/while/body/eval_jaxpr/xcdkb,dkbj->xcbj/dot_general | solution.py:44
  177.5 0.8 constant_dynamic-update-slice_fusion.2
  178.3 57.1 %all-gather.2.cloned.1.call-done = bf16[3,3,1024,256]{2,3,1,0:T(8,128)(2,1)} async-done(((bf16[3,3,1024,64]{2,3,1,0:T(8,128)(2,1)}), bf16[3,3,1024,256]{2,3,1,0:T(8,128)(2,1)}) %all-gather.2.cloned.1.call-update) | async-done | bytes 4718608 | tf_op jit(solution)/shard_map/all_gather | solution.py:64
  235.4 7.1 %fusion.15 = f32[3,256,768,1]{2,1,3,0:T(8,128)S(1)} fusion(bf16[3,3,1024,256]{2,3,1,0:T(8,128)(2,1)} %all-gather.2.cloned.1.call-done, bf16[3,1024,768]{2,1,0:T(8,128)(2,1)} %param.10), kind=kOutput, calls=%fused_computation.13 | convolution fusion | flops 3623878656 | bytes 11796480 | tf_op jit(solution)/shard_map/dot_general | solution.py:71
  242.5 2.0 copy.33
  244.5 36.4 %reduce-scatter.4.cloned.1.call-done = f32[96,768]{1,0:T(8,128)} async-done(((f32[768,768]{1,0:T(8,128)}), f32[96,768]{1,0:T(8,128)}) %reduce-scatter.4.cloned.1.call-update) | async-done | bytes 294928
  280.9 1.1 copy.34
  (45 shorter events, 4.4 us)
Async XLA Ops:
  6.5 228.8 %all-gather.2.cloned.1.call-start = ((), (), s32[]{:S(2)}) async-start(), calls=%async_computation.1 | async-start | bytes 5898240 | tf_op jit(solution)/shard_map/all_gather | solution.py:64
  7.5 24.0 %collective-permute-start = (bf16[3,256,64]{1,2,0:T(8,128)(2,1)S(1)}, bf16[3,256,64]{1,2,0:T(8,128)(2,1)S(1)}, u32[]{:S(2)}, u32[]{:S(2)}) collective-permute-start(bf16[3,256,64]{1,2,0:T(8,128)(2,1)S(1)} %get-tuple-element.115), channel_id=1, source_target_pairs={{0,1},{1,2},{2,3},{3,4},{4,5},{5,6},{6,7},{7,0},{8,9},{9,10},{10,1... | collective-permute-start | bytes 294920 | tf_op jit(solution)/shard_map/ppermute | solution.py:18
  8.0 23.5 %collective-permute-start.1 = (bf16[3,256,64]{1,2,0:T(8,128)(2,1)S(1)}, bf16[3,256,64]{1,2,0:T(8,128)(2,1)S(1)}, u32[]{:S(2)}, u32[]{:S(2)}) collective-permute-start(bf16[3,256,64]{1,2,0:T(8,128)(2,1)S(1)} %get-tuple-element.116), channel_id=1, source_target_pairs={{1,0},{2,1},{3,2},{4,3},{5,4},{6,5},{7,6},{0,7},{9,8},{10,9},{11,1... | collective-permute-start | bytes 294920 | tf_op jit(solution)/shard_map/ppermute | solution.py:21
  12.1 6.2 %copy-start.3 = (s32[1024]{0:T(1024)S(1)}, s32[1024]{0:T(1024)}, u32[]{:S(2)}) copy-start(s32[1024]{0:T(1024)} %param.15) | copy-start | bytes 12292
  12.1 6.2 %copy-start.1 = (f32[3,16,1024]{2,1,0:T(8,128)S(1)}, f32[3,16,1024]{2,1,0:T(8,128)}, u32[]{:S(2)}) copy-start(f32[3,16,1024]{2,1,0:T(8,128)} %param.13) | copy-start | bytes 589828
  19.2 12.3 %copy-start.2 = (s32[16,1024]{1,0:T(8,128)S(1)}, s32[16,1024]{1,0:T(8,128)}, u32[]{:S(2)}) copy-start(s32[16,1024]{1,0:T(8,128)} %param.14) | copy-start | bytes 196612
  19.2 12.4 %copy-start = (bf16[3,1024,64]{1,2,0:T(8,128)(2,1)S(1)}, bf16[3,1024,64]{1,2,0:T(8,128)(2,1)}, u32[]{:S(2)}) copy-start(bf16[3,1024,64]{1,2,0:T(8,128)(2,1)} %param.11) | copy-start | bytes 1179652
  178.3 102.6 %reduce-scatter.4.cloned.1.call-start = ((), (), s32[]{:S(2)}) async-start(), calls=%async_computation.2 | async-start | bytes 2654208
  242.4 2.0 copy-start.5
  242.5 2.0 copy-start.4
Sparse Core Ops, SparseCore 0:
  178.4 56.9 all-gather.1
  244.6 36.2 reduce-scatter.3
where the time goes:
time: 290 us
  local copies, waits for them, and re-layouts  133 us (46%)
  waiting for transfers between devices  93.5 us (32%)
  matrix products  31.5 us (11%)
  between operations  13.6 us (5%)
  other arithmetic  13.1 us (5%)
  starting transfers between devices  4.65 us (2%)
    gather x4, local copies, waits for them, and re-layouts, one_block(): nearby = extended[:, near_index, :]  115 us
    all_gather x1, waiting for transfers between devices, per_device(): lax.all_gather(apply_flux(extended, blocks, local_index), 'modes', axis=3...  57.1 us
    unnamed x3, waiting for transfers between devices  36.4 us
    dot_general x4, matrix products, one_block(): jnp.einsum('xcdkb,dkbj->xcbj', coefficient, nearby, preferred_element_typ...  24.4 us
    convert_element_type x1, other arithmetic, operator_blocks(): (scaled[:, None, None, :, :] * force_blocks[None]).astype(jnp.bfloat16)  12.3 us
    unnamed x15, local copies, waits for them, and re-layouts  9.3 us
    dot_general x1, matrix products, per_device(): lax.dot_general(left_flat, flux_flat, (((0,), (1,)), ((), ())), preferred...  7.07 us
  transfers between devices with their start and end apart: 4, of which 2 were waited for; matrix products, arithmetic and copies ran while one was open for 7% of the time, Pallas kernels for 0%

commit v1 on v0

v1 whole, which is shorter than its diff:
```python
import functools

import jax
import jax.numpy as jnp
from jax import lax
from jax.experimental import pallas as pl
from jax.experimental.pallas import tpu as pltpu
from jax.sharding import PartitionSpec as P

omega_step = 0.05
gamma = 0.1
F32, BF16 = jnp.float32, jnp.bfloat16
MESH = pl.DeviceIdType.MESH
NT = (((1,), (1,)), ((), ()))


def kernel(
    nm, na,
    rt, left, force, bond, nbr, counts, lbins, rbins, out,
    rx, lv, mat, lt, nrow, flux, cacc, csend, crecv, zsend, zrecv, own,
    g_send, g_recv, h_send, h_recv, c_send, c_recv, z_send, z_recv, l_sem, o_sem,
):
    slots, atoms = nbr.shape
    cols = rt.shape[1]
    halo = atoms // 4
    blocks = atoms // halo
    win = 3 * halo
    sub = lt.shape[1]
    per = lt.shape[2] // slots
    wide = lt.shape[2]
    rows = lbins.shape[0]
    nz = na // 2
    panel = cols * nm
    nl = left.shape[2]
    total_atoms = atoms * na
    m = lax.axis_index("modes")
    a = lax.axis_index("atoms")
    core = lax.rem(a, 2)
    z = a // 2
    up, down = lax.rem(a + 1, na), lax.rem(a + na - 1, na)
    sibling = a + 1 - 2 * core

    def at(mode, atom):
        return {"modes": mode, "atoms": atom}

    barrier = pltpu.get_barrier_semaphore()
    friends = [at(lax.rem(m + p, nm), a) for p in range(1, nm)]
    friends += [at(m, up), at(m, down)]
    friends += [at(m, lax.rem(a + 2 * q, na)) for q in range(1, nz)]
    for friend in friends:
        pl.semaphore_signal(barrier, inc=1, device_id=friend, device_id_type=MESH)
    lcopies = [
        pltpu.make_async_copy(left.at[c], lv.at[pl.ds(c * atoms, atoms)], l_sem.at[c])
        for c in range(3)
    ]
    for copy in lcopies:
        copy.start()
    pl.semaphore_wait(barrier, len(friends))

    my_rows = pl.ds(pl.multiple_of(m * cols, cols), cols)
    pieces = ((0, halo), (atoms - halo, halo), (halo, atoms - 2 * halo))

    def gather(p, i):
        lane, count = pieces[i]
        return pltpu.make_async_remote_copy(
            src_ref=rt.at[:, :, pl.ds(lane, count)],
            dst_ref=rx.at[:, my_rows, pl.ds(halo + lane, count)],
            send_sem=g_send.at[p - 1, i],
            recv_sem=g_recv.at[p - 1, i],
            device_id=at(lax.rem(m + p, nm), a),
            device_id_type=MESH,
        )

    def edge(p, i):
        lane = pieces[i][0]
        who = lax.rem(m + nm - p, nm)
        its_rows = pl.ds(pl.multiple_of(who * cols, cols), cols)
        src = rt.at[:, :, pl.ds(lane, halo)] if p == 0 else rx.at[:, its_rows, pl.ds(halo + lane, halo)]
        return pltpu.make_async_remote_copy(
            src_ref=src,
            dst_ref=rx.at[:, its_rows, pl.ds(halo + atoms if i == 0 else 0, halo)],
            send_sem=h_send.at[p, i],
            recv_sem=h_recv.at[p, i],
            device_id=at(m, down if i == 0 else up),
            device_id_type=MESH,
        )

    own_copy = pltpu.make_async_copy(rt, rx.at[:, my_rows, pl.ds(halo, atoms)], o_sem)
    own_copy.start()
    for i in range(3):
        for p in range(1, nm):
            gather(p, i).start()
        if i < 2:
            edge(0, i).start()

    lane_id = lax.broadcasted_iota(jnp.int32, (sub, wide), 1)
    row_id = lax.broadcasted_iota(jnp.int32, (sub, wide), 0)
    diag = lax.rem(row_id, per) == lax.rem(lane_id, per)
    k_row = lax.broadcasted_iota(jnp.int32, (128, wide), 0)
    k_lane = lax.broadcasted_iota(jnp.int32, (128, wide), 1) // per
    groups_128 = 128 // slots

    def build(u, carry):
        t = u // (halo // sub)
        r0 = lax.rem(u, halo // sub) * sub
        lanes = pl.ds(pl.multiple_of(u * sub, sub), sub)
        slot_ids = lax.broadcasted_iota(jnp.int32, (slots, sub), 0)
        live = (slot_ids < counts[:, lanes]).astype(F32)
        parts = []
        for x in range(3):
            scaled = bond[x, :, lanes] * live
            for cd in range(9):
                parts.append(scaled * force[cd, :, lanes])
        rel = nbr[:, lanes] - (a * atoms + t * halo - halo)
        rel = jnp.where(rel < 0, rel + total_atoms, rel)
        rel = jnp.where(rel >= total_atoms, rel - total_atoms, rel)
        parts.append((rel // 16).astype(F32))
        parts.append(lax.rem(rel, 16).astype(F32))
        while len(parts) % groups_128:
            parts.append(jnp.zeros((slots, sub), F32))
        spread = []
        for s in range(len(parts) // groups_128):
            block = jnp.concatenate(parts[s * groups_128:(s + 1) * groups_128], axis=0)
            spread.append(block.T.astype(BF16))

        def expand(i):
            chosen = (k_row == lax.rem(i, groups_128) * slots + k_lane).astype(F32).astype(BF16)
            return lax.dot_general(
                spread[i // groups_128], chosen, (((1,), (0,)), ((), ())),
                preferred_element_type=F32,
            )

        for i in range(27):
            lt[i] = jnp.where(diag, expand(i), 0.0).astype(BF16)
        index = jnp.where(diag, 16.0 * expand(27) + expand(28), 0.0)
        nrow[...] = jnp.sum(index.reshape(sub // per, per, wide), axis=1)

        def group(g, carry2):
            row = nrow[pl.ds(g, 1), :]
            here = pl.ds(pl.multiple_of(g * per, per), per)
            there = pl.ds(pl.multiple_of(r0 + g * per, per), per)
            lhs = lt[:, here, :].reshape(27 * per, wide)
            for n in range(3):
                b = lax.broadcasted_iota(jnp.int32, (halo, wide), 0).astype(F32) + float(n * halo)
                hot = (b == row).astype(F32).astype(BF16)
                res = lax.dot_general(lhs, hot, NT, preferred_element_type=F32).astype(BF16)
                res = res.reshape(9, 3, per, halo)
                for d in range(3):
                    mat[t, :, there, pl.ds(d * win + n * halo, halo)] = res[:, d]
            return carry2

        lax.fori_loop(0, sub // per, group, 0)
        return carry

    units = atoms // sub
    first = units // 2
    lax.fori_loop(0, first, build, 0)
    for i in range(2):
        for p in range(1, nm):
            gather(p, i).wait_recv()
            edge(p, i).start()
    lax.fori_loop(first, units, build, 0)
    own_copy.wait()
    for p in range(1, nm):
        gather(p, 2).wait_recv()
    for i in range(2):
        for p in range(nm):
            edge(p, i).wait_recv()
    for copy in lcopies:
        copy.wait()

    def cross(x):
        return pltpu.make_async_remote_copy(
            src_ref=csend.at[x], dst_ref=crecv.at[x],
            send_sem=c_send.at[x], recv_sem=c_recv.at[x],
            device_id=at(m, sibling), device_id_type=MESH,
        )

    def along(x, s):
        return pltpu.make_async_remote_copy(
            src_ref=zsend.at[x, s - 1], dst_ref=zrecv.at[x, s - 1],
            send_sem=z_send.at[x, s - 1], recv_sem=z_recv.at[x, s - 1],
            device_id=at(m, lax.rem(a + 2 * s, na)), device_id_type=MESH,
        )

    def owner_rows(o):
        return pl.ds(pl.multiple_of(o * rows, 8), rows)

    def forward(x):
        cross(x).wait_recv()
        for s in [*range(1, nz), 0]:
            q = lax.rem(z + s, nz)
            both = cacc[x % 2, owner_rows(2 * q + core), :] + crecv[x, q, :rows, :].astype(F32)
            if s:
                zsend[x, s - 1, :rows, :] = both.astype(BF16)
                along(x, s).start()
            else:
                own[x] = both

    for x in range(3):
        def one_flux(i, carry, x=x):
            c, t = i // blocks, lax.rem(i, blocks)
            acc = jnp.zeros((panel, halo), F32)
            for d in range(3):
                acc += lax.dot_general(
                    rx[d, :, pl.ds(pl.multiple_of(t * halo, halo), win)],
                    mat[t, 3 * x + c, :, pl.ds(d * win, win)],
                    NT, preferred_element_type=F32,
                )
            flux[:, pl.ds(pl.multiple_of(i * halo, halo), halo)] = acc.astype(BF16)
            return carry

        mid = blocks
        lax.fori_loop(0, mid, one_flux, 0)
        if x:
            forward(x - 1)
        lax.fori_loop(mid, 3 * blocks, one_flux, 0)

        def one_coupling(n, carry, x=x):
            lanes = pl.ds(pl.multiple_of(n * 256, 256), 256)
            part = jnp.dot(flux[...], lv[:, lanes], preferred_element_type=F32)
            cacc[x % 2, lanes, :] = part.T
            return carry

        lax.fori_loop(0, nl // 256, one_coupling, 0)
        for q in range(nz):
            csend[x, q, :rows, :] = cacc[x % 2, owner_rows(2 * q + 1 - core), :].astype(BF16)
        cross(x).start()
    forward(2)

    squares = jnp.zeros((rows, panel), F32)
    for x in range(3):
        total = own[x]
        for s in range(1, nz):
            along(x, s).wait_recv()
            total += zrecv[x, s - 1, :rows, :].astype(F32)
        squares += total * total
    omega_left = omega_step * lbins[...].astype(F32)
    omega_right = omega_step * rbins[...].astype(F32)
    gap = omega_left - omega_right
    weight = gamma * gamma / (gap * gap + gamma * gamma)
    both = omega_left + omega_right
    weight = weight * (both * both) / (4.0 * omega_left * omega_right)
    out[...] = 4.0 * jnp.sum(weight * squares, axis=1, keepdims=True) / (total_atoms * panel)

    for i in range(3):
        for p in range(1, nm):
            gather(p, i).wait_send()
    for i in range(2):
        for p in range(nm):
            edge(p, i).wait_send()
    for x in range(3):
        cross(x).wait_send()
        for s in range(1, nz):
            along(x, s).wait_send()


def per_device(
    nm, na,
    left_modes, right_panel, force_blocks, bond_vectors, neighbours, counts, left_bins, right_bins
):
    atoms, cols = right_panel.shape[1:]
    slots = neighbours.shape[0]
    nl = left_modes.shape[2]
    rows = left_bins.shape[0]
    panel = cols * nm
    halo = atoms // 4
    sub, wide = 128, 256
    nz = na // 2
    padded = -(-rows // 16) * 16
    vm = pl.BlockSpec(memory_space=pltpu.VMEM)
    hbm = pl.BlockSpec(memory_space=pl.ANY)
    dma = pltpu.SemaphoreType.DMA
    result = pl.pallas_call(
        functools.partial(kernel, nm, na),
        out_shape=jax.ShapeDtypeStruct((rows, 1), F32),
        in_specs=[hbm, hbm, vm, vm, vm, vm, vm, vm],
        out_specs=vm,
        scratch_shapes=[
            pltpu.VMEM((3, panel, atoms + 2 * halo), BF16),
            pltpu.VMEM((3 * atoms, nl), BF16),
            pltpu.VMEM((atoms // halo, 9, halo, 9 * halo), BF16),
            pltpu.VMEM((27, sub, wide), BF16),
            pltpu.VMEM((sub * slots // wide, wide), F32),
            pltpu.VMEM((panel, 3 * atoms), BF16),
            pltpu.VMEM((2, nl, panel), F32),
            pltpu.VMEM((3, nz, padded, panel), BF16),
            pltpu.VMEM((3, nz, padded, panel), BF16),
            pltpu.VMEM((3, nz - 1, padded, panel), BF16),
            pltpu.VMEM((3, nz - 1, padded, panel), BF16),
            pltpu.VMEM((3, rows, panel), F32),
            dma((nm - 1, 3)), dma((nm - 1, 3)),
            dma((nm, 2)), dma((nm, 2)),
            dma((3,)), dma((3,)),
            dma((3, nz - 1)), dma((3, nz - 1)),
            dma((3,)), dma,
        ],
        compiler_params=pltpu.CompilerParams(
            collective_id=0, has_side_effects=True, vmem_limit_bytes=60 * 2**20
        ),
    )(
        jnp.transpose(right_panel, (0, 2, 1)), left_modes,
        force_blocks.reshape(9, slots, atoms), bond_vectors, neighbours,
        counts[None, :], left_bins[:, None], right_bins[None, :],
    )
    return result[:, 0]


def solution(mesh):
    return jax.shard_map(
        functools.partial(per_device, mesh.shape["modes"], mesh.shape["atoms"]),
        mesh=mesh,
        in_specs=(
            P(None, "atoms", "modes"),
            P(None, "atoms", "modes"),
            P(None, None, None, "atoms"),
            P(None, None, "atoms"),
            P(None, "atoms"),
            P("atoms"),
            P(("modes", "atoms")),
            P(),
        ),
        out_specs=P(("modes", "atoms")),
        check_vma=False,
    )
```

time: 290 us -> 71.9 us (0.25)
  local copies, waits for them, and re-layouts: 133 us -> 1.37 us
  waiting for transfers between devices: 93.5 us -> 0 us
  Pallas kernels: 0 us -> 68.1 us
  matrix products: 31.5 us -> 0 us
  between operations: 13.6 us -> 0.01 us
  other arithmetic: 13.1 us -> 1.43 us
  starting transfers between devices: 4.65 us -> 0 us
    gather x4 -> x0, local copies, waits for them, and re-layouts: 115 us -> none  [one_block(): nearby = extended[:, near_index, :]]
    pallas_call x0 -> x1, Pallas kernels: none -> 68.1 us  [per_device(): pl.pallas_call(functools.partial(kernel, nm, na), out_shape=jax.ShapeDtyp...]
    all_gather x1 -> x0, waiting for transfers between devices: 57.1 us -> none  [per_device(): lax.all_gather(apply_flux(extended, blocks, local_index), 'modes', axis=3...]
    unnamed x3 -> x0, waiting for transfers between devices: 36.4 us -> none
    dot_general x5 -> x0, matrix products: 31.5 us -> none  [the longest x4 24.4 us: one_block(): jnp.einsum('xcdkb,dkbj->xcbj', coefficient, nearby, preferred_element_typ...]
    convert_element_type x2 -> x0, other arithmetic: 12.3 us -> none  [the longest x1 12.3 us: operator_blocks(): (scaled[:, None, None, :, :] * force_blocks[None]).astype(jnp.bfloat16)]
    unnamed x15 -> x0, local copies, waits for them, and re-layouts: 9.3 us -> none
    dynamic_update_slice x8 -> x0, local copies, waits for them, and re-layouts: 5.13 us -> none  [one_block(): lax.dynamic_update_slice_in_dim(flux_all, block_flux.astype(jnp.bfloat16)...]
  transfers between devices with their start and end apart: 4 -> 0, of which waited for: 2 -> 0; matrix products, arithmetic and copies ran while one was open for 7% -> 0% of each run, Pallas kernels for 0% -> 0%
where the time goes in v1:
time: 71.9 us; the launch traced here: 70.9 us
  Pallas kernels  68.1 us (95%)
  other arithmetic  1.43 us (2%)
  local copies, waits for them, and re-layouts  1.37 us (2%)
    pallas_call x1, Pallas kernels, per_device(): pl.pallas_call(functools.partial(kernel, nm, na), out_shape=jax.ShapeDtyp...  68.1 us

profile of v1, /device:TPU:0, one launch (start us, length us, event | category | flops | bytes accessed | tf_op | source)
XLA Modules:
  0.0 70.9 jit_solution(2670270615649100736)
XLA Ops:
  0.0 1.4 %copy.10.lbins = s32[96,1]{1,0:T(8,128)} copy(s32[96,1]{0,1:T(1,128)} %bitcast.9) | data formatting | bytes 768 | tf_op jit(solution)/shard_map/broadcast_in_dim | solution.py:304
  1.4 68.1 %shard_map.82 = f32[96,1]{1,0:T(8,128)} custom-call(bf16[3,64,1024]{2,1,0:T(8,128)(2,1)} %bitcast.6, bf16[3,1024,768]{2,1,0:T(8,128)(2,1)} %left.1, f32[9,16,1024]{2,1,0:T(8,128)} %bitcast.5, f32[3,16,1024]{2,1,0:T(8,128)} %bond.1, s32[16,1024]{1,0:T(8,128)} %nbr.1, s32[1,1024]{1,0:T(1,128)} %bitcast.7, s32[96,1]{1,0:T(8,128)} %copy.10.lbins, s32[1,256]{1,0:T(1,128)} %bitcast.8), custom_call_target="tpu_custom_call" | custom-call | tf_op jit(solution)/shard_map/pallas_call | solution.py:274
  69.5 1.4 %reduce = f32[96]{0:T(128)} reduce(f32[96,1]{1,0:T(8,128)} %shard_map.82, f32[]{:T(128)} %constant), dimensions={1}, to_apply=%pallas_call.3.reduce_sub_computation | reduce | bytes 772 | tf_op jit(solution)/shard_map/pallas_call | solution.py:274

commit v2 on v1

--- a/solution.py
+++ b/solution.py
@@ -17,7 +17,7 @@
 def kernel(
     nm, na,
     rt, left, force, bond, nbr, counts, lbins, rbins, out,
-    rx, lv, mat, lt, nrow, flux, cacc, csend, crecv, zsend, zrecv, own,
+    rx, lv, mat, lt, flux, cacc, csend, crecv, zsend, zrecv, own,
     g_send, g_recv, h_send, h_recv, c_send, c_recv, z_send, z_recv, l_sem, o_sem,
 ):
     slots, atoms = nbr.shape
@@ -28,7 +28,7 @@
     sub = lt.shape[1]
     per = lt.shape[2] // slots
     wide = lt.shape[2]
-    rows = lbins.shape[0]
+    rows = lbins.shape[1]
     nz = na // 2
     panel = cols * nm
     nl = left.shape[2]
@@ -99,6 +99,8 @@
     k_row = lax.broadcasted_iota(jnp.int32, (128, wide), 0)
     k_lane = lax.broadcasted_iota(jnp.int32, (128, wide), 1) // per
     groups_128 = 128 // slots
+    b_lane = lax.broadcasted_iota(jnp.int32, (wide, halo), 1).astype(F32).astype(BF16)
+    one, zero = jnp.ones((wide, halo), BF16), jnp.zeros((wide, halo), BF16)
 
     def build(u, carry):
         t = u // (halo // sub)
@@ -133,23 +135,19 @@
         for i in range(27):
             lt[i] = jnp.where(diag, expand(i), 0.0).astype(BF16)
         index = jnp.where(diag, 16.0 * expand(27) + expand(28), 0.0)
-        nrow[...] = jnp.sum(index.reshape(sub // per, per, wide), axis=1)
-
-        def group(g, carry2):
-            row = nrow[pl.ds(g, 1), :]
-            here = pl.ds(pl.multiple_of(g * per, per), per)
+        nrow = jnp.sum(index.reshape(sub // per, per, wide), axis=1).T
+        for g in range(sub // per):
+            column = jnp.broadcast_to(nrow[:, g:g + 1], (wide, 128))
             there = pl.ds(pl.multiple_of(r0 + g * per, per), per)
-            lhs = lt[:, here, :].reshape(27 * per, wide)
+            lhs = lt[:, g * per:(g + 1) * per, :].reshape(27 * per, wide)
             for n in range(3):
-                b = lax.broadcasted_iota(jnp.int32, (halo, wide), 0).astype(F32) + float(n * halo)
-                hot = (b == row).astype(F32).astype(BF16)
-                res = lax.dot_general(lhs, hot, NT, preferred_element_type=F32).astype(BF16)
+                near = (column - float(n * halo)).astype(BF16)
+                near = jnp.concatenate([near] * (halo // 128), axis=1)
+                hot = jnp.where(near == b_lane, one, zero)
+                res = jnp.dot(lhs, hot, preferred_element_type=F32).astype(BF16)
                 res = res.reshape(9, 3, per, halo)
                 for d in range(3):
                     mat[t, :, there, pl.ds(d * win + n * halo, halo)] = res[:, d]
-            return carry2
-
-        lax.fori_loop(0, sub // per, group, 0)
         return carry
 
     units = atoms // sub
@@ -236,12 +234,12 @@
             total += zrecv[x, s - 1, :rows, :].astype(F32)
         squares += total * total
     omega_left = omega_step * lbins[...].astype(F32)
-    omega_right = omega_step * rbins[...].astype(F32)
+    omega_right = omega_step * jnp.broadcast_to(rbins[...].astype(F32), (8, panel)).T[:, :1]
     gap = omega_left - omega_right
     weight = gamma * gamma / (gap * gap + gamma * gamma)
     both = omega_left + omega_right
     weight = weight * (both * both) / (4.0 * omega_left * omega_right)
-    out[...] = 4.0 * jnp.sum(weight * squares, axis=1, keepdims=True) / (total_atoms * panel)
+    out[...] = 4.0 * jnp.sum(weight * squares.T, axis=0, keepdims=True) / (total_atoms * panel)
 
     for i in range(3):
         for p in range(1, nm):
@@ -273,7 +271,7 @@
     dma = pltpu.SemaphoreType.DMA
     result = pl.pallas_call(
         functools.partial(kernel, nm, na),
-        out_shape=jax.ShapeDtypeStruct((rows, 1), F32),
+        out_shape=jax.ShapeDtypeStruct((1, rows), F32),
         in_specs=[hbm, hbm, vm, vm, vm, vm, vm, vm],
         out_specs=vm,
         scratch_shapes=[
@@ -281,7 +279,6 @@
             pltpu.VMEM((3 * atoms, nl), BF16),
             pltpu.VMEM((atoms // halo, 9, halo, 9 * halo), BF16),
             pltpu.VMEM((27, sub, wide), BF16),
-            pltpu.VMEM((sub * slots // wide, wide), F32),
             pltpu.VMEM((panel, 3 * atoms), BF16),
             pltpu.VMEM((2, nl, panel), F32),
             pltpu.VMEM((3, nz, padded, panel), BF16),
@@ -301,9 +298,9 @@
     )(
         jnp.transpose(right_panel, (0, 2, 1)), left_modes,
         force_blocks.reshape(9, slots, atoms), bond_vectors, neighbours,
-        counts[None, :], left_bins[:, None], right_bins[None, :],
+        counts[None, :], left_bins[None, :], right_bins[None, :],
     )
-    return result[:, 0]
+    return result.reshape(rows)
 
 
 def solution(mesh):

time: 71.9 us -> 62.7 us (0.87); the launches traced: 70.9 us -> 62.5 us
  Pallas kernels: 68.1 us -> 61.3 us
  other arithmetic: 1.43 us -> 0 us
    pallas_call x1, Pallas kernels: 68.1 us -> 61.3 us  [per_device(): pl.pallas_call(functools.partial(kernel, nm, na), out_shape=jax.ShapeDtyp...]
    pallas_call x1 -> x0, other arithmetic: 1.43 us -> none  [per_device(): pl.pallas_call(functools.partial(kernel, nm, na), out_shape=jax.ShapeDtyp...]
    broadcast_in_dim x1 -> x0, local copies, waits for them, and re-layouts: 1.37 us -> none  [per_device(): left_bins[:, None]]
    unnamed x0 -> x1, local copies, waits for them, and re-layouts: none -> 1.19 us
where the time goes in v2:
time: 62.7 us; the launch traced here: 62.5 us
  Pallas kernels  61.3 us (98%)
  local copies, waits for them, and re-layouts  1.19 us (2%)
    pallas_call x1, Pallas kernels, per_device(): pl.pallas_call(functools.partial(kernel, nm, na), out_shape=jax.ShapeDtyp...  61.3 us

profile of v2, /device:TPU:0, one launch (start us, length us, event | category | flops | bytes accessed | tf_op | source)
XLA Modules:
  0.0 62.5 jit_solution(7981254830154886117)
XLA Ops:
  0.0 61.3 %shard_map.82 = f32[1,96]{1,0:T(1,128)} custom-call(bf16[3,64,1024]{2,1,0:T(8,128)(2,1)} %bitcast.7, bf16[3,1024,768]{2,1,0:T(8,128)(2,1)} %left.1, f32[9,16,1024]{2,1,0:T(8,128)} %bitcast.6, f32[3,16,1024]{2,1,0:T(8,128)} %bond.1, s32[16,1024]{1,0:T(8,128)} %nbr.1, s32[1,1024]{1,0:T(1,128)} %bitcast.8, s32[1,96]{1,0:T(1,128)} %bitcast.10, s32[1,256]{1,0:T(1,128)} %bitcast.9), custom_call_target="tpu_custom_call" | custom-call | tf_op jit(solution)/shard_map/pallas_call | solution.py:272
  61.3 1.2 %copy.10 = f32[96]{0:T(128)} copy(f32[96]{0:T(128)} %bitcast.11) | data formatting | bytes 768

commit v3 on v2

--- a/solution.py
+++ b/solution.py
@@ -198,21 +198,17 @@
     for x in range(3):
         def one_flux(i, carry, x=x):
             c, t = i // blocks, lax.rem(i, blocks)
-            acc = jnp.zeros((panel, halo), F32)
-            for d in range(3):
-                acc += lax.dot_general(
-                    rx[d, :, pl.ds(pl.multiple_of(t * halo, halo), win)],
-                    mat[t, 3 * x + c, :, pl.ds(d * win, win)],
-                    NT, preferred_element_type=F32,
-                )
+            near = pl.ds(pl.multiple_of(t * halo, halo), win)
+            lhs = jnp.concatenate([rx[d, :, near] for d in range(3)], axis=1)
+            acc = lax.dot_general(lhs, mat[t, 3 * x + c], NT, preferred_element_type=F32)
             flux[:, pl.ds(pl.multiple_of(i * halo, halo), halo)] = acc.astype(BF16)
             return carry
 
         mid = blocks
-        lax.fori_loop(0, mid, one_flux, 0)
+        lax.fori_loop(0, mid, one_flux, 0, unroll=True)
         if x:
             forward(x - 1)
-        lax.fori_loop(mid, 3 * blocks, one_flux, 0)
+        lax.fori_loop(mid, 3 * blocks, one_flux, 0, unroll=True)
 
         def one_coupling(n, carry, x=x):
             lanes = pl.ds(pl.multiple_of(n * 256, 256), 256)

time: 62.7 us -> 57.1 us (0.911)
  Pallas kernels: 61.3 us -> 55.7 us
    pallas_call x1, Pallas kernels: 61.3 us -> 55.7 us  [per_device(): pl.pallas_call(functools.partial(kernel, nm, na), out_shape=jax.ShapeDtyp...]
where the time goes in v3:
time: 57.1 us; the launch traced here: 56.9 us
  Pallas kernels  55.7 us (98%)
  local copies, waits for them, and re-layouts  1.19 us (2%)
    pallas_call x1, Pallas kernels, per_device(): pl.pallas_call(functools.partial(kernel, nm, na), out_shape=jax.ShapeDtyp...  55.7 us
    unnamed x1, local copies, waits for them, and re-layouts  1.19 us

profile of v3, /device:TPU:0, one launch (start us, length us, event | category | flops | bytes accessed | tf_op | source)
XLA Modules:
  0.0 56.9 jit_solution(17602431782507245007)
XLA Ops:
  0.0 55.7 %shard_map.82 = f32[1,96]{1,0:T(1,128)} custom-call(bf16[3,64,1024]{2,1,0:T(8,128)(2,1)} %bitcast.7, bf16[3,1024,768]{2,1,0:T(8,128)(2,1)} %left.1, f32[9,16,1024]{2,1,0:T(8,128)} %bitcast.6, f32[3,16,1024]{2,1,0:T(8,128)} %bond.1, s32[16,1024]{1,0:T(8,128)} %nbr.1, s32[1,1024]{1,0:T(1,128)} %bitcast.8, s32[1,96]{1,0:T(1,128)} %bitcast.10, s32[1,256]{1,0:T(1,128)} %bitcast.9), custom_call_target="tpu_custom_call" | custom-call | tf_op jit(solution)/shard_map/pallas_call | solution.py:268
  55.7 1.2 %copy.10 = f32[96]{0:T(128)} copy(f32[96]{0:T(128)} %bitcast.11) | data formatting | bytes 768
